TPU v7x, 32 devices: a whole 2x2x4 slice. The times are simulated.
32 devices in a mesh: section: 8 (over z, x), tensor: 4 (over y, core).
Axes of the slice: x: 2, y: 2, z: 4, core: 2. Of those that a mesh axis runs over, the one named last changes fastest.
Arguments:
- old_query: bfloat16 [8, 4096, 4096], P('section', 'tensor'), may hold values from -0.09375 to 0.09375
- old_key: bfloat16 [8, 4096, 1024], P('section', 'tensor'), may hold values from -0.09375 to 0.09375
- old_value: bfloat16 [8, 4096, 1024], P('section', 'tensor'), may hold values from -0.09375 to 0.09375
- depth_mix: float32 [8], replicated, may hold values from -2 to 2
- width_query: bfloat16 [8192, 4096], P('section', 'tensor'), may hold values from -0.09375 to 0.09375
- width_kv: bfloat16 [1024, 1024], P('section', 'tensor'), may hold values from -0.1875 to 0.1875
- width_stream: bfloat16 [8192, 4096], P('tensor', 'section'), may hold values from -0.0625 to 0.0625
- hidden: bfloat16 [2048, 8192], P('section', 'tensor'), may hold values from -8 to 8
Outputs:
- grown_query: bfloat16 [8192, 8192], P('tensor', 'section')
- grown_key: bfloat16 [8192, 1024], P('tensor', 'section')
- grown_value: bfloat16 [8192, 1024], P('tensor', 'section')
- attended: bfloat16 [2048, 8192], P('tensor', 'section')
All inputs are finite; a program needn't handle non-finite values.
Results may differ from a plain program's by a relative error of at most 0.034.
Values may be sent and summed in bfloat16 or wider, within the bound.
A program may use at most 128 MiB of HBM per device.

v0:
```python
import math

import jax
import jax.numpy as jnp
from jax import lax
from jax.sharding import PartitionSpec as P

HD = 128
KVH = 8


def contract_last(left_side, right_side):
    return lax.dot_general(
        left_side, right_side, (((1,), (1,)), ((), ())), preferred_element_type=jnp.float32
    )


def mix_layers(depth_mix, stacked):
    flattened = stacked.reshape(stacked.shape[0], -1)
    mixed = jnp.dot(
        depth_mix, flattened, precision=lax.Precision.HIGHEST, preferred_element_type=jnp.float32
    )
    return mixed.reshape(stacked.shape[1:]).astype(jnp.bfloat16)


def pick_heads(wide, kv_ids):
    row_count = wide.shape[0]
    grouped = wide.reshape(row_count, KVH, HD)
    chosen = jnp.take(grouped, kv_ids, axis=1)
    return chosen.reshape(row_count, kv_ids.shape[0] * HD)


def per_device(
    old_query, old_key, old_value, depth_mix, width_query, width_kv, width_stream, hidden
):
    section_index = lax.axis_index("section")
    tensor_index = lax.axis_index("tensor")
    tensor_count = lax.axis_size("tensor")
    moved_query, moved_key, moved_value = (
        lax.all_to_all(old_query, "section", split_axis=2, concat_axis=0, tiled=True),
        lax.all_to_all(old_key, "section", split_axis=2, concat_axis=0, tiled=True),
        lax.all_to_all(old_value, "section", split_axis=2, concat_axis=0, tiled=True),
    )
    part_query = mix_layers(depth_mix, moved_query)
    part_key = mix_layers(depth_mix, moved_key)
    part_value = mix_layers(depth_mix, moved_value)
    mixed_query, mixed_key, mixed_value = (
        lax.all_gather(part_query, "section", axis=1, tiled=True),
        lax.all_gather(part_key, "section", axis=1, tiled=True),
        lax.all_gather(part_value, "section", axis=1, tiled=True),
    )
    query_width, kv_width = (
        lax.all_gather(width_query, "tensor", axis=1, tiled=True),
        lax.all_gather(width_kv, "tensor", axis=1, tiled=True),
    )
    expanded_query = contract_last(mixed_query, query_width).astype(jnp.bfloat16)
    expanded_key = contract_last(mixed_key, kv_width).astype(jnp.bfloat16)
    expanded_value = contract_last(mixed_value, kv_width).astype(jnp.bfloat16)
    whole_query, whole_key, whole_value = (
        lax.all_gather(expanded_query, "tensor", axis=0, tiled=True),
        lax.all_gather(expanded_key, "tensor", axis=0, tiled=True),
        lax.all_gather(expanded_value, "tensor", axis=0, tiled=True),
    )
    fragment = lax.all_gather(width_stream, "section", axis=1, tiled=True)

    def product_of(whole):
        return jnp.dot(fragment, whole, preferred_element_type=jnp.float32)

    sum_query = product_of(whole_query)
    sum_key = product_of(whole_key)
    sum_value = product_of(whole_value)
    grown_query = sum_query.astype(jnp.bfloat16)
    grown_key = sum_key.astype(jnp.bfloat16)
    grown_value = sum_value.astype(jnp.bfloat16)
    all_hidden = lax.all_gather(hidden, "section", axis=0, tiled=True)
    token_count = all_hidden.shape[0]
    block_rows = token_count // tensor_count
    query_cols = grown_query.shape[1]
    heads_here = query_cols // HD
    head_ids = section_index * heads_here + jnp.arange(heads_here, dtype=jnp.int32)
    kv_ids = head_ids % KVH
    joined = jnp.concatenate([grown_query, grown_key, grown_value], axis=1)
    summed = lax.psum_scatter(
        jnp.dot(all_hidden, joined, preferred_element_type=jnp.float32),
        "tensor",
        scatter_dimension=0,
        tiled=True,
    )
    kv_cols = (summed.shape[1] - query_cols) // 2
    queries = summed[:, :query_cols].astype(jnp.bfloat16)
    key_part = summed[:, query_cols : query_cols + kv_cols].astype(jnp.bfloat16)
    value_part = summed[:, query_cols + kv_cols :].astype(jnp.bfloat16)
    key_wide, value_wide = (
        lax.all_gather(key_part, "section", axis=1, tiled=True),
        lax.all_gather(value_part, "section", axis=1, tiled=True),
    )
    key_here = pick_heads(key_wide, kv_ids)
    value_here = pick_heads(value_wide, kv_ids)
    key_rows, value_rows = (
        lax.all_gather(key_here, "tensor", axis=0, tiled=True),
        lax.all_gather(value_here, "tensor", axis=0, tiled=True),
    )
    query_heads = queries.reshape(block_rows, heads_here, HD)
    key_heads = key_rows.reshape(token_count, heads_here, HD)
    value_heads = value_rows.reshape(token_count, heads_here, HD)
    scores = jnp.einsum(
        "qhd,khd->hqk", query_heads, key_heads, preferred_element_type=jnp.float32
    ) * (1.0 / math.sqrt(HD))
    query_position = tensor_index * block_rows + lax.broadcasted_iota(jnp.int32, (block_rows, 1), 0)
    key_position = lax.broadcasted_iota(jnp.int32, (1, token_count), 1)
    scores = jnp.where((key_position <= query_position)[None], scores, -jnp.inf)
    row_max = jnp.max(scores, axis=2, keepdims=True)
    weights = jnp.exp(scores - row_max)
    denominator = jnp.sum(weights, axis=2, keepdims=True)
    probs = weights.astype(jnp.bfloat16)
    mixed_out = (
        jnp.einsum("hqk,khd->hqd", probs, value_heads, preferred_element_type=jnp.float32)
        / denominator
    )
    attended = (
        jnp.transpose(mixed_out, (1, 0, 2))
        .reshape(block_rows, heads_here * HD)
        .astype(jnp.bfloat16)
    )
    return (grown_query, grown_key, grown_value, attended)


def solution(mesh):
    placed = (
        P("section", "tensor", None),
        P("section", "tensor", None),
        P("section", "tensor", None),
        P(),
        P("section", "tensor"),
        P("section", "tensor"),
        P("tensor", "section"),
        P("section", "tensor"),
    )
    return jax.shard_map(
        per_device,
        mesh=mesh,
        in_specs=placed,
        out_specs=(
            P("tensor", "section"),
            P("tensor", "section"),
            P("tensor", "section"),
            P("tensor", "section"),
        ),
        check_vma=False,
    )
```

profile of v0, /device:TPU:21, one launch (start us, length us, event | category | flops | bytes accessed | tf_op | source)
XLA Modules:
  0.0 1359.2 jit_solution(11355993600791226557)
XLA Ops:
  7.2 10.7 copy.34
  18.4 12.8 reduce.1
  40.6 10.7 copy.36
  51.3 14.2 %reduce.2 = bf16[1024,1024]{1,0:T(8,128)(2,1)} reduce(bf16[1024,1,1024]{2,1,0:T(2,128)(2,1)} %bitcast.111, bf16[]{:T(256)} %broadcast.70), dimensions={1}, to_apply=%bitcast.83.reduce_sub_computation | reduce | bytes 4194306
  71.8 13.2 all-to-all-done.1
  114.1 33.0 %all-to-all-done.2 = bf16[8,2,65536]{2,1,0:T(2,128)(2,1)S(1)} async-done(((bf16[8,2,65536]{2,1,0:T(2,128)(2,1)}), bf16[8,2,65536]{2,1,0:T(2,128)(2,1)S(1)}, u32[]{:S(2)}, u32[]{:S(2)}) %all-to-all-start.2) | async-done | bytes 2097184 | tf_op jit(solution)/shard_map/all_to_all | solution.py:42
  161.6 36.7 %copy.32 = bf16[1,1024,4096]{1,0,2:T(2,128)(2,1)} copy(bf16[1,1024,4096]{2,1,0:T(8,128)(2,1)} %param.10) | data formatting | bytes 16777216 | tf_op args[0]
  198.4 49.6 %reduce = bf16[4096,1024]{1,0:T(8,128)(2,1)} reduce(bf16[4096,1,1024]{2,1,0:T(2,128)(2,1)} %bitcast.105, bf16[]{:T(256)} %broadcast.70), dimensions={1}, to_apply=%bitcast.79.reduce_sub_computation | reduce | bytes 16777218
  248.0 11.3 reshape.118
  259.2 7.9 all-to-all-start
  268.3 177.5 %all-to-all-done = bf16[8,2,262144]{2,1,0:T(2,128)(2,1)} async-done(((bf16[8,2,262144]{2,1,0:T(2,128)(2,1)}), bf16[8,2,262144]{2,1,0:T(2,128)(2,1)}, u32[]{:S(2)}, u32[]{:S(2)}) %all-to-all-start) | async-done | bytes 8388640 | tf_op jit(solution)/shard_map/all_to_all | solution.py:40
  445.8 13.3 reshape.119
  459.0 12.1 copy.49
  471.1 11.4 copy.33
  482.5 13.4 fusion.23
  497.3 8.0 all_gather.47
  512.5 112.5 %all-gather.14.cloned.1.call-done = bf16[1024,4096]{1,0:T(8,128)(2,1)} async-done(((bf16[1024,512]{1,0:T(8,128)(2,1)}), bf16[1024,4096]{1,0:T(8,128)(2,1)}) %all-gather.14.cloned.1.call-update) | async-done | bytes 8388624 | tf_op jit(solution)/shard_map/all_gather | solution.py:48
  625.0 14.7 %convolution_convert_fusion.2 = bf16[1024,1024]{1,0:T(8,128)(2,1)} fusion(bf16[1024,4096]{1,0:T(8,128)(2,1)} %all-gather.14.cloned.1.call-done, bf16[1024,4096]{1,0:T(8,128)(2,1)} %all-gather.16.cloned.1.call-done), kind=kOutput, calls=%fused_computation.30 | convolution fusion | flops 8590983168 | bytes 18874368 | tf_op jit(solution)/shard_map/dot_general | solution.py:13
  642.8 228.9 %all-gather.20.cloned.1.call-done = bf16[2048,4096]{1,0:T(8,128)(2,1)} async-done(((bf16[2048,512]{1,0:T(8,128)(2,1)}), bf16[2048,4096]{1,0:T(8,128)(2,1)}) %all-gather.20.cloned.1.call-update) | async-done | bytes 16777232 | tf_op jit(solution)/shard_map/all_gather | solution.py:64
  871.7 11.8 fusion.11
  889.5 11.8 fusion.12
  901.4 48.6 %all-gather.18.cloned.1.call-done = bf16[4096,1024]{1,0:T(8,128)(2,1)} async-done(((bf16[1024,1024]{1,0:T(8,128)(2,1)}), bf16[4096,1024]{1,0:T(8,128)(2,1)}) %all-gather.18.cloned.1.call-update) | async-done | bytes 8388624 | tf_op jit(solution)/shard_map/all_gather | solution.py:60
  950.0 24.1 %convert_bitcast_fusion = bf16[2048,1024]{0,1:T(8,128)(2,1)} fusion(bf16[4096,1024]{1,0:T(8,128)(2,1)} %all-gather.18.cloned.1.call-done, bf16[2048,4096]{1,0:T(8,128)(2,1)} %all-gather.20.cloned.1.call-done), kind=kOutput, calls=%fused_computation.16 | convolution fusion | flops 17181966336 | bytes 29360128 | tf_op jit(solution)/shard_map/dot_general | solution.py:67
  974.1 102.2 %all-gather.30.cloned.1.call-done = bf16[2048,2048]{1,0:T(8,128)(2,1)} async-done(((bf16[256,2048]{1,0:T(8,128)(2,1)}), bf16[2048,2048]{1,0:T(8,128)(2,1)}) %all-gather.30.cloned.1.call-update) | async-done | bytes 8388624 | tf_op jit(solution)/shard_map/all_gather | solution.py:75
  1076.3 17.2 %convolution_bitcast_fusion = f32[2048,1280]{0,1:T(8,128)} fusion(bf16[2048,2048]{1,0:T(8,128)(2,1)} %all-gather.30.cloned.1.call-done, bf16[2048,128]{0,1:T(8,128)(2,1)S(1)} %fusion.12, bf16[2048,128]{0,1:T(8,128)(2,1)S(1)} %fusion.11, bf16[2048,1024]{0,1:T(8,128)(2,1)} %convert_bitcast_fusion), kind=kOutput, calls=%fused_computation.9 | convolution fusion | flops 10753146880 | bytes 24117248 | tf_op jit(solution)/shard_map/dot_general | solution.py:84
  1093.5 84.0 %reduce-scatter.2.cloned.1.call-done = f32[512,1280]{0,1:T(8,128)} async-done(((f32[2048,1280]{0,1:T(8,128)}), f32[512,1280]{0,1:T(8,128)}) %reduce-scatter.2.cloned.1.call-update) | async-done | bytes 2621456 | tf_op jit(solution)/shard_map/reduce_scatter | solution.py:83
  1180.9 38.4 %all-gather.32.cloned.1.call-done = bf16[512,1024]{0,1:T(8,128)(2,1)} async-done(((bf16[512,128]{0,1:T(8,128)(2,1)}), bf16[512,1024]{0,1:T(8,128)(2,1)}) %all-gather.32.cloned.1.call-update) | async-done | bytes 1048592 | tf_op jit(solution)/shard_map/all_gather | solution.py:94
  1221.1 39.7 %all-gather.36.cloned.1.call-done = bf16[512,1024]{0,1:T(8,128)(2,1)} async-done(((bf16[512,128]{0,1:T(8,128)(2,1)}), bf16[512,1024]{0,1:T(8,128)(2,1)}) %all-gather.36.cloned.1.call-update) | async-done | bytes 1048592 | tf_op jit(solution)/shard_map/all_gather | solution.py:95
  1276.4 22.9 %all-gather.34.cloned.1.call-done = bf16[2048,1024]{0,1:T(8,128)(2,1)} async-done(((bf16[512,1024]{0,1:T(8,128)(2,1)}), bf16[2048,1024]{0,1:T(8,128)(2,1)}) %all-gather.34.cloned.1.call-update) | async-done | bytes 4194320 | tf_op jit(solution)/shard_map/all_gather | solution.py:100
  1299.3 17.5 %fusion = (f32[8,512]{1,0:T(8,128)S(1)}, f32[8,512,2048]{2,1,0:T(8,128)}) fusion(pred[512,2048]{1,0:T(8,128)(4,1)S(1)} %iota_compare_fusion, bf16[512,8,128]{0,2,1:T(8,128)(2,1)S(1)} %bitcast.117, bf16[2048,8,128]{0,2,1:T(8,128)(2,1)} %bitcast.112), kind=kOutput, calls=%fused_computation.4 | convolution fusion | flops 2172645376 | bytes 39862272 | tf_op jit(solution)/shard_map/qhd,khd->hqk/dot_general | solution.py:106
  1316.8 15.1 %fusion.1 = f32[8,512]{1,0:T(8,128)S(1)} fusion(f32[8,512,2048]{2,1,0:T(8,128)} %get-tuple-element.26, f32[8,512]{1,0:T(8,128)S(1)} %get-tuple-element.25, pred[512,2048]{1,0:T(8,128)(4,1)S(1)} %iota_compare_fusion), kind=kLoop, calls=%fused_computation.5 | loop fusion | flops 33550336 | bytes 34635776 | tf_op jit(solution)/shard_map/reduce_sum | solution.py:114
  1335.2 15.7 %fusion.17 = bf16[512,8,128]{0,2,1:T(8,128)(2,1)S(1)} fusion(bf16[2048,8,128]{0,2,1:T(8,128)(2,1)} %bitcast.127, f32[8,512,2048]{2,1,0:T(8,128)} %get-tuple-element.26, f32[8,512]{1,0:T(8,128)S(1)} %get-tuple-element.25, pred[512,2048]{1,0:T(8,128)(4,1)S(1)} %iota_compare_fusion, f32[512,8]{0,1:T(8,128)S(1)} %bitcast.126), kind=kOutput, calls=%fused_computation.28 | convolution fusion | flops 2182086656 | bytes 39878656 | tf_op jit(solution)/shard_map/hqk,khd->hqd/dot_general | solution.py:117
  (79 shorter events, 103.8 us)
Async XLA Ops:
  7.2 101.8 %copy-start = (f32[8]{0:T(128)S(1)}, f32[8]{0:T(128)}, u32[]{:S(2)}) copy-start(f32[8]{0:T(128)} %param.13) | copy-start | bytes 100
  35.0 50.0 %all-to-all-start.1 = ((bf16[8,2,65536]{2,1,0:T(2,128)(2,1)}), bf16[8,2,65536]{2,1,0:T(2,128)(2,1)S(1)}, u32[]{:S(2)}, u32[]{:S(2)}) async-start(bf16[8,2,65536]{2,1,0:T(2,128)(2,1)} %reshape.120), calls=%async_computation.1 | async-start | bytes 4194304 | tf_op jit(solution)/shard_map/all_to_all | solution.py:41
  85.0 1.3 copy-start.2
  86.3 60.7 %all-to-all-start.2 = ((bf16[8,2,65536]{2,1,0:T(2,128)(2,1)}), bf16[8,2,65536]{2,1,0:T(2,128)(2,1)S(1)}, u32[]{:S(2)}, u32[]{:S(2)}) async-start(bf16[8,2,65536]{2,1,0:T(2,128)(2,1)} %reshape.122), calls=%async_computation.2 | async-start | bytes 4194304 | tf_op jit(solution)/shard_map/all_to_all | solution.py:42
  94.0 411.3 %all-gather.22.cloned.1.call-start = ((), (), s32[]{:S(2)}) async-start(), calls=%async_computation.8 | async-start | bytes 2359296 | tf_op jit(solution)/shard_map/all_gather | solution.py:49
  113.8 395.2 %all-gather.26.cloned.1.call-start = ((), (), s32[]{:S(2)}) async-start(), calls=%async_computation.10 | async-start | bytes 2359296 | tf_op jit(solution)/shard_map/all_gather | solution.py:50
  259.2 186.5 %all-to-all-start = ((bf16[8,2,262144]{2,1,0:T(2,128)(2,1)}), bf16[8,2,262144]{2,1,0:T(2,128)(2,1)}, u32[]{:S(2)}, u32[]{:S(2)}) async-start(bf16[8,2,262144]{2,1,0:T(2,128)(2,1)} %reshape.118), calls=%async_computation | async-start | bytes 16777216 | tf_op jit(solution)/shard_map/all_to_all | solution.py:40
  267.1 245.4 %all-gather.16.cloned.1.call-start = ((), (), s32[]{:S(2)}) async-start(), calls=%async_computation.5 | async-start | bytes 10485760 | tf_op jit(solution)/shard_map/all_gather | solution.py:53
  267.9 357.2 %all-gather.14.cloned.1.call-start = ((), (), s32[]{:S(2)}) async-start(), calls=%async_computation.4 | async-start | bytes 9437184 | tf_op jit(solution)/shard_map/all_gather | solution.py:48
  482.5 14.7 %copy-start.5 = (bf16[128,256]{1,0:T(8,128)(2,1)S(1)}, bf16[128,256]{1,0:T(8,128)(2,1)}, u32[]{:S(2)}) copy-start(bf16[128,256]{1,0:T(8,128)(2,1)} %param.15) | copy-start | bytes 196612
  497.2 145.5 %all-gather.24.cloned.1.call-start = ((), (), s32[]{:S(2)}) async-start(), calls=%async_computation.9 | async-start | bytes 1310720 | tf_op jit(solution)/shard_map/all_gather | solution.py:61
  508.3 363.3 %all-gather.20.cloned.1.call-start = ((), (), s32[]{:S(2)}) async-start(), calls=%async_computation.7 | async-start | bytes 18874368 | tf_op jit(solution)/shard_map/all_gather | solution.py:64
  508.9 380.6 %all-gather.28.cloned.1.call-start = ((), (), s32[]{:S(2)}) async-start(), calls=%async_computation.11 | async-start | bytes 1310720 | tf_op jit(solution)/shard_map/all_gather | solution.py:62
  512.3 437.7 %all-gather.18.cloned.1.call-start = ((), (), s32[]{:S(2)}) async-start(), calls=%async_computation.6 | async-start | bytes 10485760 | tf_op jit(solution)/shard_map/all_gather | solution.py:60
  639.8 436.5 %all-gather.30.cloned.1.call-start = ((), (), s32[]{:S(2)}) async-start(), calls=%async_computation.12 | async-start | bytes 9437184 | tf_op jit(solution)/shard_map/all_gather | solution.py:75
  640.5 537.0 %reduce-scatter.2.cloned.1.call-start = ((), (), s32[]{:S(2)}) async-start(), calls=%async_computation.13 | async-start | bytes 13107200 | tf_op jit(solution)/shard_map/reduce_scatter | solution.py:83
  883.5 192.8 %copy-start.3 = (bf16[2048,128]{0,1:T(8,128)(2,1)}, bf16[2048,128]{0,1:T(8,128)(2,1)S(1)}, u32[]{:S(2)}) copy-start(bf16[2048,128]{0,1:T(8,128)(2,1)S(1)} %fusion.11) | copy-start | bytes 1572868
  901.4 174.9 %copy-start.4 = (bf16[2048,128]{0,1:T(8,128)(2,1)}, bf16[2048,128]{0,1:T(8,128)(2,1)S(1)}, u32[]{:S(2)}) copy-start(bf16[2048,128]{0,1:T(8,128)(2,1)S(1)} %fusion.12) | copy-start | bytes 1572868
  1093.5 125.8 %all-gather.32.cloned.1.call-start = ((), (), s32[]{:S(2)}) async-start(), calls=%async_computation.14 | async-start | bytes 1179648 | tf_op jit(solution)/shard_map/all_gather | solution.py:94
  1180.2 80.6 %all-gather.36.cloned.1.call-start = ((), (), s32[]{:S(2)}) async-start(), calls=%async_computation.16 | async-start | bytes 1179648 | tf_op jit(solution)/shard_map/all_gather | solution.py:95
  1180.8 118.5 %all-gather.34.cloned.1.call-start = ((), (), s32[]{:S(2)}) async-start(), calls=%async_computation.15 | async-start | bytes 5242880 | tf_op jit(solution)/shard_map/all_gather | solution.py:100
  1264.3 71.0 %all-gather.38.cloned.1.call-start = ((), (), s32[]{:S(2)}) async-start(), calls=%async_computation.17 | async-start | bytes 5242880 | tf_op jit(solution)/shard_map/all_gather | solution.py:101
  1335.2 17.0 %copy-start.1 = (f32[8]{0:T(128)S(1)}, f32[8]{0:T(128)}, u32[]{:S(2)}) copy-start(f32[8]{0:T(128)} %param.13) | copy-start | bytes 100
Sparse Core Ops, SparseCore 0:
  113.9 60.0 all-gather.21
  176.6 49.2 all-gather.25
  269.5 59.7 all-gather.15
  497.3 127.6 all-gather.13
  627.0 15.6 all-gather.23
  644.7 226.9 all-gather.19
  873.8 15.6 all-gather.27
  891.7 58.3 all-gather.17
  952.1 124.1 all-gather.29
  1093.6 83.8 reduce-scatter.1
  1180.3 38.9 all-gather.31
  1221.8 38.8 all-gather.35
  1264.4 34.8 all-gather.33
  1300.7 34.4 all-gather.37
where the time goes:
time: 1370 us; the launch traced here: 1360 us
  waiting for transfers between devices  916 us (67%)
  local copies, waits for them, and re-layouts  161 us (12%)
  matrix products  141 us (10%)
  other arithmetic  97.3 us (7%)
  starting transfers between devices  22.4 us (2%)
  between operations  14.5 us (1%)
    all_gather x1, waiting for transfers between devices, per_device(): fragment = lax.all_gather(width_stream, 'section', axis=1, tiled=True)  229 us
    all_to_all x1, waiting for transfers between devices, per_device(): lax.all_to_all(old_query, 'section', split_axis=2, concat_axis=0, tiled=T...  177 us
    unnamed x29, local copies, waits for them, and re-layouts  137 us
    all_gather x1, waiting for transfers between devices, per_device(): lax.all_gather(part_query, 'section', axis=1, tiled=True)  113 us
    all_gather x1, waiting for transfers between devices, per_device(): all_hidden = lax.all_gather(hidden, 'section', axis=0, tiled=True)  102 us
    reduce_scatter x1, waiting for transfers between devices, per_device(): lax.psum_scatter(jnp.dot(all_hidden, joined, preferred_element_type=jnp.f...  84 us
    unnamed x3, other arithmetic  76.5 us
    all_gather x1, waiting for transfers between devices, per_device(): lax.all_gather(expanded_query, 'tensor', axis=0, tiled=True)  48.6 us
  transfers between devices with their start and end apart: 17, of which 14 were waited for; matrix products, arithmetic and copies ran while one was open for 24% of the time, Pallas kernels for 0%

commit v1 on v0

--- a/solution.py
+++ b/solution.py
@@ -1,17 +1,877 @@
+import functools
 import math
 
 import jax
 import jax.numpy as jnp
 from jax import lax
+from jax.experimental import pallas as pl
+from jax.experimental.pallas import tpu as pltpu
 from jax.sharding import PartitionSpec as P
 
 HD = 128
 KVH = 8
+MIB = 1024 * 1024
+ANY = pl.BlockSpec(memory_space=pl.ANY)
 
 
 def contract_last(left_side, right_side):
     return lax.dot_general(
         left_side, right_side, (((1,), (1,)), ((), ())), preferred_element_type=jnp.float32
+    )
+
+
+def remote(src, dst, send, recv, axis, index):
+    return pltpu.make_async_remote_copy(
+        src_ref=src,
+        dst_ref=dst,
+        send_sem=send,
+        recv_sem=recv,
+        device_id={axis: index},
+        device_id_type=pl.DeviceIdType.MESH,
+    )
+
+
+class Place:
+    def __init__(self, sections):
+        self.count = sections // 2
+        self.section = lax.axis_index("section")
+        self.tensor = lax.axis_index("tensor")
+        self.z = self.section // 2
+        self.x = self.section % 2
+        self.y = self.tensor // 2
+        self.core = self.tensor % 2
+        self.other_x = self.z * 2 + 1 - self.x
+        self.other_y = (1 - self.y) * 2 + self.core
+        self.other_core = self.y * 2 + 1 - self.core
+
+
+class SectionGather:
+    def __init__(self, place, own, view, sems, local_sem=None, on_block=None, wide=False):
+        self.p = place
+        self.own = view(place.section) if own is None else own
+        self.view = view
+        self.sems = sems
+        self.local = None
+        if local_sem is not None:
+            self.local = pltpu.make_async_copy(self.own, view(place.section), local_sem)
+        self.on_block = on_block
+        self.wide = wide
+
+    def copy(self, kind, origin, src):
+        p = self.p
+        target = (p.section + 2, p.section - 2, p.other_x)[kind - 1]
+        return remote(
+            src,
+            self.view(origin),
+            self.sems.at[kind, origin],
+            self.sems.at[0, origin],
+            "section",
+            target,
+        )
+
+    def start_z(self):
+        p = self.p
+
+        @pl.when(p.z < p.count - 1)
+        def _():
+            self.copy(1, p.section, self.own).start()
+
+        @pl.when(p.z > 0)
+        def _():
+            self.copy(2, p.section, self.own).start()
+
+        if self.local is not None:
+            self.local.start()
+
+    def start_x(self):
+        self.copy(3, self.p.section, self.own).start()
+
+    def start(self):
+        if self.wide:
+            self.start_x()
+            self.start_z()
+        else:
+            self.start_z()
+            self.start_x()
+
+    def arrived(self, origin):
+        self.copy(3, origin, self.view(origin)).wait_recv()
+
+    def cross(self):
+        p = self.p
+        if self.wide:
+            origin = p.other_x
+            block = self.view(origin)
+            self.arrived(origin)
+
+            @pl.when(p.z < p.count - 1)
+            def _():
+                self.copy(1, origin, block).start()
+
+            @pl.when(p.z > 0)
+            def _():
+                self.copy(2, origin, block).start()
+
+    def step(self, hop):
+        p = self.p
+
+        def take(origin, kind, more):
+            block = self.view(origin)
+            self.arrived(origin)
+
+            @pl.when(more)
+            def _():
+                self.copy(kind, origin, block).start()
+
+            if not self.wide:
+                self.copy(3, origin, block).start()
+            if self.on_block is not None:
+                self.on_block(origin)
+
+        columns = (p.section, p.other_x) if self.wide else (p.section,)
+
+        @pl.when(p.z - hop >= 0)
+        def _():
+            for column in columns:
+                take(column - 2 * hop, 1, p.z < p.count - 1)
+
+        @pl.when(p.z + hop < p.count)
+        def _():
+            for column in columns:
+                take(column + 2 * hop, 2, p.z > 0)
+
+    def finish(self):
+        p = self.p
+        if self.local is not None:
+            self.local.wait()
+        if not self.wide:
+            for other_z in range(p.count):
+                across = other_z * 2 + 1 - p.x
+                self.arrived(across)
+                if self.on_block is not None:
+                    self.on_block(across)
+        for other_z in range(p.count):
+            for column in (p.x, 1 - p.x) if self.wide else (p.x,):
+                origin = other_z * 2 + column
+                block = self.view(origin)
+
+                @pl.when((other_z <= p.z) & (p.z < p.count - 1))
+                def _():
+                    self.copy(1, origin, block).wait_send()
+
+                @pl.when((other_z >= p.z) & (p.z > 0))
+                def _():
+                    self.copy(2, origin, block).wait_send()
+
+            if not self.wide:
+                self.copy(3, origin, block).wait_send()
+        if self.wide:
+            self.copy(3, p.section, self.own).wait_send()
+
+
+class TensorGather:
+    def __init__(self, place, own, view, sems, local_sem):
+        p = place
+        mine, far = p.tensor, p.other_y
+        self.local = pltpu.make_async_copy(own, view(mine), local_sem)
+        self.to_y = remote(own, view(mine), sems.at[0], sems.at[1], "tensor", p.other_y)
+        self.to_core = remote(own, view(mine), sems.at[2], sems.at[3], "tensor", p.other_core)
+        self.far_to_core = remote(
+            view(far), view(far), sems.at[4], sems.at[5], "tensor", p.other_core
+        )
+
+    def start(self):
+        self.to_y.start()
+        self.to_core.start()
+        self.local.start()
+
+    def forward(self):
+        self.to_y.wait_recv()
+        self.far_to_core.start()
+
+    def finish(self):
+        self.local.wait()
+        self.to_y.wait_send()
+        self.to_core.wait()
+        self.far_to_core.wait()
+
+
+PARTS = 2
+
+
+def mix_kernel(
+    sections,
+    depth_mix,
+    old_query,
+    old_key,
+    old_value,
+    width_query,
+    width_kv,
+    width_stream,
+    mixed_query,
+    mixed_key,
+    mixed_value,
+    query_width,
+    kv_width,
+    fragment,
+    held,
+    peer,
+    sums,
+    up,
+    down,
+    mine,
+    load_sems,
+    pair_sems,
+    ring_sems,
+    mixed_sems,
+    stream_sems,
+    width_sems,
+    local_sems,
+):
+    p = Place(sections)
+    count = p.count
+    rows = held.shape[1]
+    part_rows = rows // PARTS
+    q_cols = old_query.shape[1] // sections
+    k_cols = old_key.shape[1] // sections
+    fields = (
+        (old_query, 0, q_cols),
+        (old_key, q_cols, k_cols),
+        (old_value, q_cols + k_cols, k_cols),
+    )
+    factor = depth_mix[p.section]
+    peer_factor = depth_mix[p.other_x]
+
+    def pair_copies(far):
+        for i, (ref, first, width) in enumerate(fields):
+            start = pl.multiple_of((far * 2 + 1 - p.x) * width, 128)
+            yield remote(
+                ref.at[:, pl.ds(start, width)],
+                peer.at[far, :, pl.ds(first, width)],
+                pair_sems.at[0, far, i],
+                pair_sems.at[1, far, i],
+                "section",
+                p.other_x,
+            )
+
+    def at_distance(distance, act):
+        @pl.when(p.z + distance < count)
+        def _():
+            act(p.z + distance)
+
+        if distance:
+
+            @pl.when(p.z - distance >= 0)
+            def _():
+                act(p.z - distance)
+
+    def send_pair(far):
+        for one in pair_copies(far):
+            one.start()
+
+    def pair_arrived(far):
+        for one in pair_copies(far):
+            one.wait_recv()
+
+    at_distance(count - 1, send_pair)
+
+    loads = []
+    for far in range(count):
+        for i, (ref, first, width) in enumerate(fields):
+            start = pl.multiple_of((far * 2 + p.x) * width, 128)
+            load = pltpu.make_async_copy(
+                ref.at[:, pl.ds(start, width)],
+                held.at[far, :, pl.ds(first, width)],
+                load_sems.at[3 * far + i],
+            )
+            load.start()
+            loads.append(load)
+
+    stream_rows, stream_cols = width_stream.shape
+    wide_rows = stream_rows // 4
+
+    def stream_gather(index, window, wide):
+        return SectionGather(
+            p,
+            width_stream.at[window],
+            lambda s: fragment.at[
+                window, pl.ds(pl.multiple_of(s * stream_cols, 128), stream_cols)
+            ],
+            stream_sems.at[index],
+            local_sems.at[index],
+            wide=wide,
+        )
+
+    wide_stream = stream_gather(0, pl.ds(0, wide_rows), True)
+    stream = stream_gather(1, pl.ds(wide_rows, stream_rows - wide_rows), False)
+    wide_cols, kv_width_cols = width_query.shape[1], width_kv.shape[1]
+    widths = [
+        TensorGather(
+            p,
+            width_query,
+            lambda t: query_width.at[:, pl.ds(pl.multiple_of(t * wide_cols, 128), wide_cols)],
+            width_sems.at[0],
+            local_sems.at[2],
+        ),
+        TensorGather(
+            p,
+            width_kv,
+            lambda t: kv_width.at[
+                :, pl.ds(pl.multiple_of(t * kv_width_cols, 128), kv_width_cols)
+            ],
+            width_sems.at[1],
+            local_sems.at[3],
+        ),
+    ]
+    for one in widths:
+        one.start()
+    wide_stream.start()
+    stream.start_z()
+
+    @pl.when(p.z == 0)
+    def _():
+        up[...] = jnp.zeros(up.shape, up.dtype)
+
+    @pl.when(p.z == count - 1)
+    def _():
+        down[...] = jnp.zeros(down.shape, down.dtype)
+
+    for load in loads:
+        load.wait()
+
+    step_rows = 32
+
+    def ring(direction, distance, part):
+        window = pl.ds(part * part_rows, part_rows)
+        target = p.section + 2 if direction == 0 else p.section - 2
+        slot = p.z + distance - 1 if direction == 0 else p.z - distance
+        return remote(
+            sums.at[slot, window],
+            (up, down)[direction].at[distance - 1, window],
+            ring_sems.at[direction, 0, distance - 1, part],
+            ring_sems.at[direction, 1, distance - 1, part],
+            "section",
+            target,
+        )
+
+    def ring_arrived(direction, distance, part):
+        slot = (up, down)[direction].at[distance - 1, pl.ds(part * part_rows, part_rows)]
+        remote(
+            slot,
+            slot,
+            ring_sems.at[direction, 0, distance - 1, part],
+            ring_sems.at[direction, 1, distance - 1, part],
+            "section",
+            p.other_x,
+        ).wait_recv()
+
+    def pair_sum(far, window):
+        value = held[far, window, :].astype(jnp.float32) * factor
+        return value + peer[far, window, :].astype(jnp.float32) * peer_factor
+
+    def relay(direction, distance, part):
+        slots = (up, down)[direction]
+        far = p.z + distance if direction == 0 else p.z - distance
+        slot = p.z + distance - 1 if direction == 0 else p.z - distance
+        sends = far < count if direction == 0 else far >= 0
+        receives = p.z > 0 if direction == 0 else p.z < count - 1
+
+        @pl.when(sends)
+        def _():
+            if distance < count - 1:
+
+                @pl.when(receives)
+                def _():
+                    ring_arrived(direction, distance + 1, part)
+
+            @pl.loop(0, part_rows // step_rows)
+            def _(i):
+                window = pl.ds(
+                    pl.multiple_of(part * part_rows + i * step_rows, step_rows), step_rows
+                )
+                value = pair_sum(far, window)
+                if distance < count - 1:
+                    value += slots[distance, window, :]
+                sums[slot, window, :] = value
+
+            if distance < count - 1:
+                beyond = far + 1 < count if direction == 0 else far - 1 >= 0
+
+                @pl.when(beyond)
+                def _():
+                    ring(direction, distance + 1, part).wait_send()
+
+            ring(direction, distance, part).start()
+
+    for distance in range(count - 1, 0, -1):
+        at_distance(distance, pair_arrived)
+        at_distance(distance - 1, send_pair)
+        if distance == 1:
+            stream.start_x()
+        for part in range(PARTS):
+            relay(0, distance, part)
+            relay(1, distance, part)
+        if distance == count - 1:
+            wide_stream.cross()
+        if distance == min(2, count - 1):
+            for one in widths:
+                one.forward()
+            wide_stream.step(1)
+            stream.step(1)
+    for hop in range(2, count - 1):
+        wide_stream.step(hop)
+        stream.step(hop)
+    at_distance(0, pair_arrived)
+
+    gathers = []
+    for part in range(PARTS):
+
+        @pl.when(p.z > 0)
+        def _():
+            ring_arrived(0, 1, part)
+
+        @pl.when(p.z < count - 1)
+        def _():
+            ring_arrived(1, 1, part)
+
+        @pl.loop(0, part_rows // step_rows)
+        def _(i):
+            window = pl.ds(pl.multiple_of(part * part_rows + i * step_rows, step_rows), step_rows)
+            value = pair_sum(p.z, window) + up[0, window, :] + down[0, window, :]
+            mine[window, :] = value.astype(jnp.bfloat16)
+
+        window = pl.ds(part * part_rows, part_rows)
+        for i, (ref, first, width) in enumerate(
+            (
+                (mixed_query, 0, q_cols),
+                (mixed_key, q_cols, k_cols),
+                (mixed_value, q_cols + k_cols, k_cols),
+            )
+        ):
+            gather = SectionGather(
+                p,
+                mine.at[window, pl.ds(first, width)],
+                lambda s, ref=ref, width=width, window=window: ref.at[
+                    window, pl.ds(pl.multiple_of(s * width, 128), width)
+                ],
+                mixed_sems.at[3 * part + i],
+                local_sems.at[4 + 3 * part + i],
+                wide=i == 0 and part == 0,
+            )
+            gather.start()
+            gathers.append(gather)
+    if count > 2:
+        wide_stream.step(count - 1)
+        stream.step(count - 1)
+    for gather in gathers:
+        gather.cross()
+    for hop in range(1, count):
+        for gather in gathers:
+            gather.step(hop)
+
+    for far in range(count):
+        for one in pair_copies(far):
+            one.wait_send()
+    for part in range(PARTS):
+
+        @pl.when(p.z < count - 1)
+        def _():
+            ring(0, 1, part).wait_send()
+
+        @pl.when(p.z > 0)
+        def _():
+            ring(1, 1, part).wait_send()
+
+    wide_stream.finish()
+    stream.finish()
+    for one in widths:
+        one.finish()
+    for gather in gathers:
+        gather.finish()
+
+
+def spread_kernel(
+    sections,
+    expanded,
+    hidden,
+    whole,
+    all_hidden,
+    expanded_sems,
+    hidden_sems,
+    local_sems,
+):
+    p = Place(sections)
+    rows, tokens = expanded.shape[0], hidden.shape[0]
+    wide = TensorGather(
+        p,
+        expanded,
+        lambda t: whole.at[pl.ds(pl.multiple_of(t * rows, 16), rows)],
+        expanded_sems,
+        local_sems.at[0],
+    )
+    wide_tokens = tokens // 8
+    states = [
+        SectionGather(
+            p,
+            hidden.at[pl.ds(first, size)],
+            lambda s, first=first, size=size: all_hidden.at[
+                pl.ds(pl.multiple_of(s * tokens + first, 16), size)
+            ],
+            hidden_sems.at[index],
+            local_sems.at[1 + index],
+            wide=index == 0,
+        )
+        for index, (first, size) in enumerate(
+            ((0, wide_tokens), (wide_tokens, tokens - wide_tokens))
+        )
+    ]
+    wide.start()
+    for one in states:
+        one.start()
+    for one in states:
+        one.cross()
+    for hop in range(1, p.count):
+        for one in states:
+            one.step(hop)
+    wide.forward()
+    for one in states:
+        one.finish()
+    wide.finish()
+
+
+def sum_kernel(
+    sections,
+    partial,
+    queries,
+    joint,
+    near,
+    from_core,
+    y_out,
+    y_in,
+    own,
+    near_sems,
+    core_sems,
+    y_sems,
+    own_y_sems,
+    joint_sems,
+    local_sems,
+    side_sems,
+):
+    p = Place(sections)
+    rows = near.shape[1]
+    q_cols = queries.shape[1]
+    joint_cols = own.shape[1]
+    spans = ((q_cols, joint_cols), (0, q_cols))
+
+    def core_copy(span, row_y):
+        first, width = spans[span]
+        block = row_y * 2 + 1 - p.core
+        return remote(
+            partial.at[pl.ds(pl.multiple_of(block * rows, 16), rows), pl.ds(first, width)],
+            from_core.at[row_y, :, pl.ds(first, width)],
+            core_sems.at[0, span, row_y],
+            core_sems.at[1, span, row_y],
+            "tensor",
+            p.other_core,
+        )
+
+    def near_copy(span, row_y):
+        first, width = spans[span]
+        block = row_y * 2 + p.core
+        return pltpu.make_async_copy(
+            partial.at[pl.ds(pl.multiple_of(block * rows, 16), rows), pl.ds(first, width)],
+            near.at[row_y, :, pl.ds(first, width)],
+            near_sems.at[span, row_y],
+        )
+
+    def y_copy(span):
+        first, width = spans[span]
+        return remote(
+            y_out.at[:, pl.ds(first, width)],
+            y_in.at[:, pl.ds(first, width)],
+            y_sems.at[0, span],
+            y_sems.at[1, span],
+            "tensor",
+            p.other_y,
+        )
+
+    step_rows = 32
+
+    def each_window(body):
+        @pl.loop(0, rows // step_rows)
+        def _(i):
+            body(pl.ds(pl.multiple_of(i * step_rows, step_rows), step_rows))
+
+    def core_sum(span, row_y, window):
+        first, width = spans[span]
+        columns = pl.ds(first, width)
+        return near[row_y, window, columns] + from_core[row_y, window, columns]
+
+    def send_sum(span):
+        first, width = spans[span]
+        near_copy(span, 1 - p.y).wait()
+        core_copy(span, 1 - p.y).wait_recv()
+
+        def body(window):
+            y_out[window, pl.ds(first, width)] = core_sum(span, 1 - p.y, window).astype(
+                jnp.bfloat16
+            )
+
+        each_window(body)
+        y_copy(span).start()
+
+    def take_sum(span, target):
+        first, width = spans[span]
+        near_copy(span, p.y).wait()
+        core_copy(span, p.y).wait_recv()
+        y_copy(span).wait_recv()
+
+        def body(window):
+            value = core_sum(span, p.y, window)
+            value += y_in[window, pl.ds(first, width)].astype(jnp.float32)
+            target[window, :] = value.astype(jnp.bfloat16)
+
+        each_window(body)
+
+    for span in range(2):
+        for row_y in (1 - p.y, p.y):
+            core_copy(span, row_y).start()
+            near_copy(span, row_y).start()
+
+    def block(t, s):
+        return joint.at[
+            pl.ds(pl.multiple_of(t * rows, 16), rows),
+            pl.ds(pl.multiple_of(s * joint_cols, 128), joint_cols),
+        ]
+
+    def side(row_y, core, s, src):
+        return remote(
+            src,
+            block(row_y * 2 + core, s),
+            side_sems.at[row_y, 0, s],
+            side_sems.at[row_y, 1, s],
+            "tensor",
+            p.other_core,
+        )
+
+    def hand_on(row_y):
+        def act(s):
+            side(row_y, p.core, s, block(row_y * 2 + p.core, s)).start()
+
+        return act
+
+    send_sum(0)
+    take_sum(0, own)
+    own_y = remote(
+        own,
+        block(p.tensor, p.section),
+        own_y_sems.at[0],
+        own_y_sems.at[1],
+        "tensor",
+        p.other_y,
+    )
+    own_y.start()
+    near_gather = SectionGather(
+        p, own, lambda s: block(p.tensor, s), joint_sems.at[0], local_sems.at[0], hand_on(p.y)
+    )
+    far_gather = SectionGather(
+        p, None, lambda s: block(p.other_y, s), joint_sems.at[1], None, hand_on(1 - p.y)
+    )
+    near_gather.start()
+    side(p.y, p.core, p.section, own).start()
+    own_y.wait_recv()
+    far_gather.start()
+    side(1 - p.y, p.core, p.section, block(p.other_y, p.section)).start()
+    send_sum(1)
+    for hop in range(1, p.count):
+        near_gather.step(hop)
+        far_gather.step(hop)
+    take_sum(1, queries)
+    near_gather.finish()
+    far_gather.finish()
+
+    @pl.loop(0, sections)
+    def _(s):
+        for row_y in range(2):
+            from_other = block(row_y * 2 + 1 - p.core, s)
+            side(row_y, 1 - p.core, s, from_other).wait_recv()
+            side(row_y, p.core, s, block(row_y * 2 + p.core, s)).wait_send()
+
+    own_y.wait_send()
+    for span in range(2):
+        y_copy(span).wait_send()
+        for row_y in (1 - p.y, p.y):
+            core_copy(span, row_y).wait_send()
+
+
+def attend_kernel(first, queries, joint, attended):
+    rows = queries.shape[0]
+    tensor_index = first[0]
+    query = queries[...]
+    scale = 1.0 / math.sqrt(HD)
+
+    def scores_of(index):
+        keys = joint[pl.ds(pl.multiple_of(index * rows, 128), rows), :HD]
+        return contract_last(query, keys) * scale
+
+    def merge(index, scores, carry):
+        top, bottom, running = carry
+        best = jnp.maximum(top, jnp.max(scores, axis=1, keepdims=True))
+        weights = jnp.exp(scores - best)
+        shrink = jnp.exp(top - best)
+        values = joint[pl.ds(pl.multiple_of(index * rows, 128), rows), HD:]
+        bottom = bottom * shrink + jnp.sum(weights, axis=1, keepdims=True)
+        running = running * shrink + jnp.dot(
+            weights.astype(jnp.bfloat16), values, preferred_element_type=jnp.float32
+        )
+        return best, bottom, running
+
+    scores = scores_of(tensor_index)
+    row_of = lax.broadcasted_iota(jnp.int32, (rows, rows), 0)
+    column_of = lax.broadcasted_iota(jnp.int32, (rows, rows), 1)
+    scores = jnp.where(column_of <= row_of, scores, -jnp.inf)
+    top = jnp.max(scores, axis=1, keepdims=True)
+    weights = jnp.exp(scores - top)
+    values = joint[pl.ds(pl.multiple_of(tensor_index * rows, 128), rows), HD:]
+    bottom = jnp.sum(weights, axis=1, keepdims=True)
+    running = jnp.dot(weights.astype(jnp.bfloat16), values, preferred_element_type=jnp.float32)
+    top, bottom, running = lax.fori_loop(
+        0,
+        tensor_index,
+        lambda index, carry: merge(index, scores_of(index), carry),
+        (top, bottom, running),
+    )
+    attended[...] = (running / bottom).astype(jnp.bfloat16)
+
+
+def attend(queries, joint, tensor_index):
+    rows, cols = queries.shape
+    tokens = joint.shape[0]
+    return pl.pallas_call(
+        attend_kernel,
+        out_shape=jax.ShapeDtypeStruct((rows, cols), jnp.bfloat16),
+        grid_spec=pltpu.PrefetchScalarGridSpec(
+            num_scalar_prefetch=1,
+            grid=(cols // HD,),
+            in_specs=[
+                pl.BlockSpec((rows, HD), lambda h, first: (0, h)),
+                pl.BlockSpec((tokens, 2 * HD), lambda h, first: (0, h % KVH)),
+            ],
+            out_specs=pl.BlockSpec((rows, HD), lambda h, first: (0, h)),
+        ),
+        compiler_params=pltpu.CompilerParams(vmem_limit_bytes=40 * MIB),
+    )(tensor_index.reshape(1).astype(jnp.int32), queries, joint)
+
+
+def fast_device(
+    old_query, old_key, old_value, depth_mix, width_query, width_kv, width_stream, hidden
+):
+    sections = lax.axis_size("section")
+    tensors = lax.axis_size("tensor")
+    count = sections // 2
+    bf16 = jnp.bfloat16
+    dma = pltpu.SemaphoreType.DMA
+    rows, model_cols = old_query.shape[1:]
+    kv_cols = old_key.shape[2]
+    seg = (model_cols + 2 * kv_cols) // sections
+    stream_rows, stream_cols = width_stream.shape
+    head_cols = width_query.shape[0]
+    kv_head_cols = width_kv.shape[0]
+
+    mixed_query, mixed_key, mixed_value, query_width, kv_width, fragment = pl.pallas_call(
+        functools.partial(mix_kernel, sections),
+        out_shape=[
+            jax.ShapeDtypeStruct((rows, model_cols), bf16),
+            jax.ShapeDtypeStruct((rows, kv_cols), bf16),
+            jax.ShapeDtypeStruct((rows, kv_cols), bf16),
+            jax.ShapeDtypeStruct((head_cols, model_cols), bf16),
+            jax.ShapeDtypeStruct((kv_head_cols, kv_cols), bf16),
+            jax.ShapeDtypeStruct((stream_rows, stream_cols * sections), bf16),
+        ],
+        in_specs=[pl.BlockSpec(memory_space=pltpu.SMEM)] + [ANY] * 6,
+        out_specs=[ANY] * 6,
+        scratch_shapes=[
+            pltpu.VMEM((count, rows, seg), bf16),
+            pltpu.VMEM((count, rows, seg), bf16),
+            pltpu.VMEM((count - 1, rows, seg), jnp.float32),
+            pltpu.VMEM((count - 1, rows, seg), jnp.float32),
+            pltpu.VMEM((count - 1, rows, seg), jnp.float32),
+            pltpu.VMEM((rows, seg), bf16),
+            dma((3 * count,)),
+            dma((2, count, 3)),
+            dma((2, 2, count - 1, PARTS)),
+            dma((3 * PARTS, 4, sections)),
+            dma((2, 4, sections)),
+            dma((2, 6)),
+            dma((4 + 3 * PARTS,)),
+        ],
+        compiler_params=pltpu.CompilerParams(
+            vmem_limit_bytes=52 * MIB, has_side_effects=True
+        ),
+    )(depth_mix, old_query[0], old_key[0], old_value[0], width_query, width_kv, width_stream)
+
+    expanded = jnp.concatenate(
+        [
+            contract_last(mixed_query, query_width).astype(bf16),
+            contract_last(mixed_key, kv_width).astype(bf16),
+            contract_last(mixed_value, kv_width).astype(bf16),
+        ],
+        axis=1,
+    )
+    joined_cols = expanded.shape[1]
+    token_part, feature_cols = hidden.shape
+    tokens = token_part * sections
+
+    whole, all_hidden = pl.pallas_call(
+        functools.partial(spread_kernel, sections),
+        out_shape=[
+            jax.ShapeDtypeStruct((rows * tensors, joined_cols), bf16),
+            jax.ShapeDtypeStruct((tokens, feature_cols), bf16),
+        ],
+        in_specs=[ANY] * 2,
+        out_specs=[ANY] * 2,
+        scratch_shapes=[dma((6,)), dma((2, 4, sections)), dma((3,))],
+        compiler_params=pltpu.CompilerParams(
+            vmem_limit_bytes=16 * MIB, has_side_effects=True
+        ),
+    )(expanded, hidden)
+
+    grown = jnp.dot(fragment, whole, preferred_element_type=jnp.float32).astype(bf16)
+    partial = jnp.dot(all_hidden, grown, preferred_element_type=jnp.float32)
+    block_rows = tokens // tensors
+    queries, joint = pl.pallas_call(
+        functools.partial(sum_kernel, sections),
+        out_shape=[
+            jax.ShapeDtypeStruct((block_rows, head_cols), bf16),
+            jax.ShapeDtypeStruct((tokens, 2 * kv_head_cols * sections), bf16),
+        ],
+        in_specs=[ANY],
+        out_specs=[pl.BlockSpec(memory_space=pltpu.VMEM), ANY],
+        scratch_shapes=[
+            pltpu.VMEM((2, block_rows, joined_cols), jnp.float32),
+            pltpu.VMEM((2, block_rows, joined_cols), jnp.float32),
+            pltpu.VMEM((block_rows, joined_cols), bf16),
+            pltpu.VMEM((block_rows, joined_cols), bf16),
+            pltpu.VMEM((block_rows, 2 * kv_head_cols), bf16),
+            dma((2, 2)),
+            dma((2, 2, 2)),
+            dma((2, 2)),
+            dma((2,)),
+            dma((2, 4, sections)),
+            dma((1,)),
+            dma((2, 2, sections)),
+        ],
+        compiler_params=pltpu.CompilerParams(
+            vmem_limit_bytes=32 * MIB, has_side_effects=True
+        ),
+    )(partial)
+
+    attended = attend(queries, joint, lax.axis_index("tensor"))
+    return (
+        grown[:, :head_cols],
+        grown[:, head_cols : head_cols + kv_head_cols],
+        grown[:, head_cols + kv_head_cols :],
+        attended,
     )
 
 
@@ -30,7 +890,7 @@
     return chosen.reshape(row_count, kv_ids.shape[0] * HD)
 
 
-def per_device(
+def plain_device(
     old_query, old_key, old_value, depth_mix, width_query, width_kv, width_stream, hidden
 ):
     section_index = lax.axis_index("section")
@@ -125,6 +985,11 @@
     return (grown_query, grown_key, grown_value, attended)
 
 
+def fits(mesh):
+    sections, tensors = mesh.shape["section"], mesh.shape["tensor"]
+    return sections == KVH and tensors == 4
+
+
 def solution(mesh):
     placed = (
         P("section", "tensor", None),
@@ -137,7 +1002,7 @@
         P("section", "tensor"),
     )
     return jax.shard_map(
-        per_device,
+        fast_device if fits(mesh) else plain_device,
         mesh=mesh,
         in_specs=placed,
         out_specs=(

time: 1370 us -> 728 us (0.53)
  waiting for transfers between devices: 916 us -> 0 us
  Pallas kernels: 0 us -> 659 us
  local copies, waits for them, and re-layouts: 161 us -> 12.7 us
  other arithmetic: 97.3 us -> 0.25 us
  matrix products: 141 us -> 54.6 us
  starting transfers between devices: 22.4 us -> 0 us
  between operations: 14.5 us -> 0.75 us
    pallas_call x0 -> x4, Pallas kernels: none -> 659 us  [the longest x1 439 us: fast_device(): pl.pallas_call(functools.partial(mix_kernel, sections), out_shape=[jax.Sh...]
    all_gather x13 -> x0, waiting for transfers between devices: 605 us -> none  [the longest x1 229 us: per_device(): fragment = lax.all_gather(width_stream, 'section', axis=1, tiled=True)]
    all_to_all x3 -> x0, waiting for transfers between devices: 224 us -> none  [the longest x1 177 us: per_device(): lax.all_to_all(old_query, 'section', split_axis=2, concat_axis=0, tiled=T...]
    unnamed x29 -> x14, local copies, waits for them, and re-layouts: 137 us -> 9.06 us
    reduce_scatter x1 -> x0, waiting for transfers between devices: 84 us -> none  [per_device(): lax.psum_scatter(jnp.dot(all_hidden, joined, preferred_element_type=jnp.f...]
    dot_general x9 -> x2, matrix products: 120 us -> 36.2 us  [the longest x1 24.8 us: fast_device(): jnp.dot(fragment, whole, preferred_element_type=jnp.float32).astype(bf16)]
    unnamed x3 -> x0, other arithmetic: 76.5 us -> none
    all_to_all x3 -> x0, starting transfers between devices: 21.2 us -> none  [the longest x1 7.9 us: per_device(): lax.all_to_all(old_query, 'section', split_axis=2, concat_axis=0, tiled=T...]
  transfers between devices with their start and end apart: 17 -> 0, of which waited for: 14 -> 0; matrix products, arithmetic and copies ran while one was open for 24% -> 0% of each run, Pallas kernels for 0% -> 0%
where the time goes in v1:
time: 728 us; the launch traced here: 727 us
  Pallas kernels  659 us (91%)
  matrix products  54.6 us (8%)
  local copies, waits for them, and re-layouts  12.7 us (2%)
    pallas_call x1, Pallas kernels, fast_device(): pl.pallas_call(functools.partial(mix_kernel, sections), out_shape=[jax.Sh...  439 us
    pallas_call x1, Pallas kernels, fast_device(): pl.pallas_call(functools.partial(spread_kernel, sections), out_shape=[jax...  116 us
    pallas_call x1, Pallas kernels, fast_device(): pl.pallas_call(functools.partial(sum_kernel, sections), out_shape=[jax.Sh...  77.5 us
    pallas_call x1, Pallas kernels, attend(): pl.pallas_call(attend_kernel, out_shape=jax.ShapeDtypeStruct((rows, cols)...  26.3 us
    dot_general x1, matrix products, fast_device(): jnp.dot(fragment, whole, preferred_element_type=jnp.float32).astype(bf16)  24.8 us
    dot_general x3, matrix products, contract_last(): lax.dot_general(left_side, right_side, (((1,), (1,)), ((), ())), preferre...  18.3 us

profile of v1, /device:TPU:21, one launch (start us, length us, event | category | flops | bytes accessed | tf_op | source)
XLA Modules:
  0.0 727.2 jit_solution(401393076200660653)
XLA Ops:
  0.6 0.0 copy-start.3
  0.6 0.8 copy-done.3
  1.5 0.0 copy-start.4
  1.5 0.7 copy-done.4
  2.1 438.8 %shard_map.111 = (bf16[1024,4096]{1,0:T(8,128)(2,1)}, bf16[1024,1024]{1,0:T(8,128)(2,1)}, bf16[1024,1024]{1,0:T(8,128)(2,1)}, bf16[1024,4096]{1,0:T(8,128)(2,1)}...) custom-call(f32[8]{0:T(128)S(1)} %copy-done.4, bf16[1024,4096]{1,0:T(8,128)(2,1)} %bitcast.14, ...), custom_call_target="tpu_custom_call" | custom-call | tf_op jit(solution)/shard_map/pallas_call | solution.py:781
  440.9 2.3 convolution_convert_fusion.3
  443.2 2.3 convolution_convert_fusion.2
  445.5 13.7 %convolution_convert_fusion.1 = bf16[1024,1024]{1,0:T(8,128)(2,1)S(1)} fusion(bf16[1024,4096]{1,0:T(8,128)(2,1)} %get-tuple-element.15, bf16[1024,4096]{1,0:T(8,128)(2,1)} %get-tuple-element.16), kind=kOutput, calls=%fused_computation.2 | convolution fusion | flops 8590983168 | bytes 18874368 | tf_op jit(solution)/shard_map/dot_general | solution.py:18
  459.3 0.0 copy-start.2
  459.3 0.2 pad_maximum_fusion.expanded
  459.5 1.0 copy-done.2
  460.5 116.4 %shard_map.112 = (bf16[4096,1280]{1,0:T(8,128)(2,1)S(1)}, bf16[2048,2048]{1,0:T(8,128)(2,1)S(1)}) custom-call(bf16[1024,1280]{1,0:T(8,128)(2,1)S(1)} %pad_maximum_fusion.expanded, bf16[256,2048]{1,0:T(8,128)(2,1)S(1)} %copy-done.2), custom_call_target="tpu_custom_call" | custom-call | tf_op jit(solution)/shard_map/pallas_call | solution.py:825
  576.9 24.8 %convolution_convert_fusion = bf16[2048,1280]{1,0:T(8,128)(2,1)S(1)} fusion(bf16[2048,4096]{1,0:T(8,128)(2,1)} %get-tuple-element.14, bf16[4096,1280]{1,0:T(8,128)(2,1)S(1)} %get-tuple-element.20), kind=kOutput, calls=%fused_computation | convolution fusion | flops 21477457920 | bytes 32505856 | tf_op jit(solution)/shard_map/dot_general | solution.py:839
  601.7 0.0 copy-start.5
  601.7 11.4 %fusion.1.partial = f32[2048,1280]{1,0:T(8,128)S(1)} fusion(bf16[2048,2048]{1,0:T(8,128)(2,1)S(1)} %get-tuple-element.21, bf16[2048,1280]{1,0:T(8,128)(2,1)S(1)} %convolution_convert_fusion), kind=kOutput, calls=%fused_computation.6 | convolution fusion | flops 10737418240 | bytes 24117248 | tf_op jit(solution)/shard_map/dot_general | solution.py:840
  613.1 0.0 copy-done.5
  613.1 77.5 %shard_map.113 = (bf16[512,1024]{1,0:T(8,128)(2,1)S(1)}, bf16[2048,2048]{1,0:T(8,128)(2,1)S(1)}) custom-call(f32[2048,1280]{1,0:T(8,128)S(1)} %fusion.1.partial), custom_call_target="tpu_custom_call" | custom-call | tf_op jit(solution)/shard_map/pallas_call | solution.py:842
  690.7 0.0 copy-start
  690.7 3.2 copy-done
  693.9 0.0 copy-start.1
  693.9 3.4 copy-done.1
  697.3 0.0 copy-start.6
  697.3 26.3 %shard_map.114 = bf16[512,1024]{1,0:T(8,128)(2,1)} custom-call(s32[1]{0:T(128)} %bitcast.3.first, bf16[512,1024]{1,0:T(8,128)(2,1)S(1)} %get-tuple-element.22.queries, bf16[2048,2048]{1,0:T(8,128)(2,1)S(1)} %copy-done.1), custom_call_target="tpu_custom_call" | custom-call | tf_op jit(solution)/shard_map/pallas_call | solution.py:750
  723.6 0.0 copy-done.6
  723.6 1.0 fusion
  724.6 2.6 slice.12
Async XLA Ops:
  0.6 0.8 copy-start.3
  1.5 0.7 copy-start.4
  459.3 1.2 copy-start.2
  601.7 11.4 %copy-start.5 = (bf16[2048,1280]{1,0:T(8,128)(2,1)}, bf16[2048,1280]{1,0:T(8,128)(2,1)S(1)}, u32[]{:S(2)}) copy-start(bf16[2048,1280]{1,0:T(8,128)(2,1)S(1)} %convolution_convert_fusion) | copy-start | bytes 15728644
  690.7 3.2 copy-start
  693.9 3.4 copy-start.1
  697.3 26.3 %copy-start.6 = (bf16[2048,1280]{1,0:T(8,128)(2,1)S(1)}, bf16[2048,1280]{1,0:T(8,128)(2,1)}, u32[]{:S(2)}) copy-start(bf16[2048,1280]{1,0:T(8,128)(2,1)} %copy-done.5) | copy-start | bytes 15728644

commit v2 on v1

--- a/solution.py
+++ b/solution.py
@@ -490,18 +490,9 @@
         gather.finish()
 
 
-def spread_kernel(
-    sections,
-    expanded,
-    hidden,
-    whole,
-    all_hidden,
-    expanded_sems,
-    hidden_sems,
-    local_sems,
-):
+def spread_kernel(sections, expanded, whole, expanded_sems, local_sems):
     p = Place(sections)
-    rows, tokens = expanded.shape[0], hidden.shape[0]
+    rows = expanded.shape[0]
     wide = TensorGather(
         p,
         expanded,
@@ -509,33 +500,8 @@
         expanded_sems,
         local_sems.at[0],
     )
-    wide_tokens = tokens // 8
-    states = [
-        SectionGather(
-            p,
-            hidden.at[pl.ds(first, size)],
-            lambda s, first=first, size=size: all_hidden.at[
-                pl.ds(pl.multiple_of(s * tokens + first, 16), size)
-            ],
-            hidden_sems.at[index],
-            local_sems.at[1 + index],
-            wide=index == 0,
-        )
-        for index, (first, size) in enumerate(
-            ((0, wide_tokens), (wide_tokens, tokens - wide_tokens))
-        )
-    ]
     wide.start()
-    for one in states:
-        one.start()
-    for one in states:
-        one.cross()
-    for hop in range(1, p.count):
-        for one in states:
-            one.step(hop)
     wide.forward()
-    for one in states:
-        one.finish()
     wide.finish()
 
 
@@ -704,44 +670,59 @@
             core_copy(span, row_y).wait_send()
 
 
+GROUP = 2
+
+
 def attend_kernel(first, queries, joint, attended):
     rows = queries.shape[0]
     tensor_index = first[0]
-    query = queries[...]
-    scale = 1.0 / math.sqrt(HD)
-
-    def scores_of(index):
-        keys = joint[pl.ds(pl.multiple_of(index * rows, 128), rows), :HD]
-        return contract_last(query, keys) * scale
-
-    def merge(index, scores, carry):
+    scale = 1.0 / math.sqrt(HD) / math.log(2.0)
+
+    def span(index):
+        return pl.ds(pl.multiple_of(index * rows, 128), rows)
+
+    def scores_of(index, i):
+        keys = joint[span(index), 2 * i * HD : (2 * i + 1) * HD]
+        return contract_last(queries[:, i * HD : (i + 1) * HD], keys)
+
+    def values_of(index, i):
+        return joint[span(index), (2 * i + 1) * HD : (2 * i + 2) * HD]
+
+    def opening(i):
+        scores = scores_of(tensor_index, i)
+        row_of = lax.broadcasted_iota(jnp.int32, (rows, rows), 0)
+        column_of = lax.broadcasted_iota(jnp.int32, (rows, rows), 1)
+        scores = jnp.where(column_of <= row_of, scores, -jnp.inf)
+        top = jnp.max(scores, axis=1, keepdims=True)
+        weights = jnp.exp2((scores - top) * scale)
+        bottom = jnp.sum(weights, axis=1, keepdims=True)
+        running = jnp.dot(
+            weights.astype(jnp.bfloat16),
+            values_of(tensor_index, i),
+            preferred_element_type=jnp.float32,
+        )
+        return top, bottom, running
+
+    def merge(index, i, carry):
         top, bottom, running = carry
+        scores = scores_of(index, i)
         best = jnp.maximum(top, jnp.max(scores, axis=1, keepdims=True))
-        weights = jnp.exp(scores - best)
-        shrink = jnp.exp(top - best)
-        values = joint[pl.ds(pl.multiple_of(index * rows, 128), rows), HD:]
+        weights = jnp.exp2((scores - best) * scale)
+        shrink = jnp.exp2((top - best) * scale)
         bottom = bottom * shrink + jnp.sum(weights, axis=1, keepdims=True)
         running = running * shrink + jnp.dot(
-            weights.astype(jnp.bfloat16), values, preferred_element_type=jnp.float32
+            weights.astype(jnp.bfloat16), values_of(index, i), preferred_element_type=jnp.float32
         )
         return best, bottom, running
 
-    scores = scores_of(tensor_index)
-    row_of = lax.broadcasted_iota(jnp.int32, (rows, rows), 0)
-    column_of = lax.broadcasted_iota(jnp.int32, (rows, rows), 1)
-    scores = jnp.where(column_of <= row_of, scores, -jnp.inf)
-    top = jnp.max(scores, axis=1, keepdims=True)
-    weights = jnp.exp(scores - top)
-    values = joint[pl.ds(pl.multiple_of(tensor_index * rows, 128), rows), HD:]
-    bottom = jnp.sum(weights, axis=1, keepdims=True)
-    running = jnp.dot(weights.astype(jnp.bfloat16), values, preferred_element_type=jnp.float32)
-    top, bottom, running = lax.fori_loop(
+    state = lax.fori_loop(
         0,
         tensor_index,
-        lambda index, carry: merge(index, scores_of(index), carry),
-        (top, bottom, running),
-    )
-    attended[...] = (running / bottom).astype(jnp.bfloat16)
+        lambda index, state: tuple(merge(index, i, one) for i, one in enumerate(state)),
+        tuple(opening(i) for i in range(GROUP)),
+    )
+    for i, (_, bottom, running) in enumerate(state):
+        attended[:, i * HD : (i + 1) * HD] = (running / bottom).astype(jnp.bfloat16)
 
 
 def attend(queries, joint, tensor_index):
@@ -752,14 +733,14 @@
         out_shape=jax.ShapeDtypeStruct((rows, cols), jnp.bfloat16),
         grid_spec=pltpu.PrefetchScalarGridSpec(
             num_scalar_prefetch=1,
-            grid=(cols // HD,),
+            grid=(cols // (GROUP * HD),),
             in_specs=[
-                pl.BlockSpec((rows, HD), lambda h, first: (0, h)),
-                pl.BlockSpec((tokens, 2 * HD), lambda h, first: (0, h % KVH)),
+                pl.BlockSpec((rows, GROUP * HD), lambda h, first: (0, h)),
+                pl.BlockSpec((tokens, 2 * GROUP * HD), lambda h, first: (0, h % (KVH // GROUP))),
             ],
-            out_specs=pl.BlockSpec((rows, HD), lambda h, first: (0, h)),
+            out_specs=pl.BlockSpec((rows, GROUP * HD), lambda h, first: (0, h)),
         ),
-        compiler_params=pltpu.CompilerParams(vmem_limit_bytes=40 * MIB),
+        compiler_params=pltpu.CompilerParams(vmem_limit_bytes=58 * MIB),
     )(tensor_index.reshape(1).astype(jnp.int32), queries, joint)
 
 
@@ -778,6 +759,7 @@
     head_cols = width_query.shape[0]
     kv_head_cols = width_kv.shape[0]
 
+    all_hidden = lax.all_gather(hidden, "section", axis=0, tiled=True)
     mixed_query, mixed_key, mixed_value, query_width, kv_width, fragment = pl.pallas_call(
         functools.partial(mix_kernel, sections),
         out_shape=[
@@ -819,22 +801,18 @@
         axis=1,
     )
     joined_cols = expanded.shape[1]
-    token_part, feature_cols = hidden.shape
-    tokens = token_part * sections
-
-    whole, all_hidden = pl.pallas_call(
+    tokens = all_hidden.shape[0]
+
+    whole = pl.pallas_call(
         functools.partial(spread_kernel, sections),
-        out_shape=[
-            jax.ShapeDtypeStruct((rows * tensors, joined_cols), bf16),
-            jax.ShapeDtypeStruct((tokens, feature_cols), bf16),
-        ],
-        in_specs=[ANY] * 2,
-        out_specs=[ANY] * 2,
-        scratch_shapes=[dma((6,)), dma((2, 4, sections)), dma((3,))],
+        out_shape=jax.ShapeDtypeStruct((rows * tensors, joined_cols), bf16),
+        in_specs=[ANY],
+        out_specs=ANY,
+        scratch_shapes=[dma((6,)), dma((1,))],
         compiler_params=pltpu.CompilerParams(
             vmem_limit_bytes=16 * MIB, has_side_effects=True
         ),
-    )(expanded, hidden)
+    )(expanded)
 
     grown = jnp.dot(fragment, whole, preferred_element_type=jnp.float32).astype(bf16)
     partial = jnp.dot(all_hidden, grown, preferred_element_type=jnp.float32)
@@ -862,7 +840,7 @@
             dma((2, 2, sections)),
         ],
         compiler_params=pltpu.CompilerParams(
-            vmem_limit_bytes=32 * MIB, has_side_effects=True
+            vmem_limit_bytes=56 * MIB, has_side_effects=True
         ),
     )(partial)
 

time: 728 us -> 809 us (1.11)
  Pallas kernels: 659 us -> 721 us
  between operations: 0.75 us -> 14.1 us
    pallas_call x1, Pallas kernels: 439 us -> 536 us  [fast_device(): pl.pallas_call(functools.partial(mix_kernel, sections), out_shape=[jax.Sh...]
    pallas_call x1, Pallas kernels: 116 us -> 94.1 us  [fast_device(): pl.pallas_call(functools.partial(spread_kernel, sections), out_shape=jax....]
    pallas_call x1, Pallas kernels: 77.5 us -> 69 us  [fast_device(): pl.pallas_call(functools.partial(sum_kernel, sections), out_shape=[jax.Sh...]
  transfers between devices with their start and end apart: 0 -> 1, of which waited for: 0 -> 0; matrix products, arithmetic and copies ran while one was open for 0% -> 6% of each run, Pallas kernels for 0% -> 78%
where the time goes in v2:
time: 809 us
  Pallas kernels  721 us (89%)
  matrix products  62.5 us (8%)
  between operations  14.1 us (2%)
  local copies, waits for them, and re-layouts  10.1 us (1%)
    pallas_call x1, Pallas kernels, fast_device(): pl.pallas_call(functools.partial(mix_kernel, sections), out_shape=[jax.Sh...  536 us
    pallas_call x1, Pallas kernels, fast_device(): pl.pallas_call(functools.partial(spread_kernel, sections), out_shape=jax....  94.1 us
    pallas_call x1, Pallas kernels, fast_device(): pl.pallas_call(functools.partial(sum_kernel, sections), out_shape=[jax.Sh...  69 us
    dot_general x1, matrix products, fast_device(): jnp.dot(fragment, whole, preferred_element_type=jnp.float32).astype(bf16)  27.6 us
    pallas_call x1, Pallas kernels, attend(): pl.pallas_call(attend_kernel, out_shape=jax.ShapeDtypeStruct((rows, cols)...  22.2 us
    dot_general x3, matrix products, contract_last(): lax.dot_general(left_side, right_side, (((1,), (1,)), ((), ())), preferre...  18.3 us
    dot_general x1, matrix products, fast_device(): partial = jnp.dot(all_hidden, grown, preferred_element_type=jnp.float32)  16.6 us
  transfers between devices with their start and end apart: 1, of which 0 were waited for; matrix products, arithmetic and copies ran while one was open for 6% of the time, Pallas kernels for 78%

profile of v2, /device:TPU:21, one launch (start us, length us, event | category | flops | bytes accessed | tf_op | source)
XLA Modules:
  0.0 809.1 jit_solution(827839308978418062)
XLA Ops:
  7.2 0.0 all-gather.2.cloned.1.call-start
  7.2 0.7 all-gather.2.cloned.1.call-update
  7.9 0.0 copy-start.1
  7.9 0.8 copy-done.1
  8.7 0.0 copy-start.2
  8.7 0.7 copy-done.2
  9.4 536.1 %shard_map.111 = (bf16[1024,4096]{1,0:T(8,128)(2,1)}, bf16[1024,1024]{1,0:T(8,128)(2,1)}, bf16[1024,1024]{1,0:T(8,128)(2,1)}, bf16[1024,4096]{1,0:T(8,128)(2,1)}...) custom-call(f32[8]{0:T(128)S(1)} %copy-done.2, bf16[1024,4096]{1,0:T(8,128)(2,1)} %bitcast.16, ...), custom_call_target="tpu_custom_call" | custom-call | tf_op jit(solution)/shard_map/pallas_call | solution.py:763
  545.5 2.3 convolution_convert_fusion.3
  547.8 2.3 convolution_convert_fusion.2
  550.2 13.7 %convolution_convert_fusion.1 = bf16[1024,1024]{1,0:T(8,128)(2,1)S(1)} fusion(bf16[1024,4096]{1,0:T(8,128)(2,1)} %get-tuple-element.13, bf16[1024,4096]{1,0:T(8,128)(2,1)} %get-tuple-element.14), kind=kOutput, calls=%fused_computation.3 | convolution fusion | flops 8590983168 | bytes 18874368 | tf_op jit(solution)/shard_map/dot_general | solution.py:18
  563.9 0.2 pad_maximum_fusion.expanded
  564.2 94.1 %shard_map.112 = bf16[4096,1280]{1,0:T(8,128)(2,1)S(1)} custom-call(bf16[1024,1280]{1,0:T(8,128)(2,1)S(1)} %pad_maximum_fusion.expanded), custom_call_target="tpu_custom_call" | custom-call | tf_op jit(solution)/shard_map/pallas_call | solution.py:806
  658.3 0.0 copy-start
  658.3 4.0 copy-done
  662.3 27.6 %convolution_convert_fusion = bf16[2048,1280]{1,0:T(8,128)(2,1)S(1)} fusion(bf16[2048,4096]{1,0:T(8,128)(2,1)} %get-tuple-element.12, bf16[4096,1280]{1,0:T(8,128)(2,1)} %copy-done), kind=kOutput, calls=%fused_computation.1 | convolution fusion | flops 21477457920 | bytes 32505856 | tf_op jit(solution)/shard_map/dot_general | solution.py:817
  689.9 0.0 copy-start.3
  689.9 3.0 slice.12
  692.8 0.6 copy-done.3
  693.5 1.0 fusion
  694.5 0.0 all-gather.2.cloned.1.call-done
  694.5 16.6 %convolution_bitcast_fusion.partial = f32[2048,1280]{1,0:T(8,128)} fusion(bf16[2048,2048]{1,0:T(8,128)(2,1)} %all-gather.2.cloned.1.call-done, bf16[2048,1280]{1,0:T(8,128)(2,1)} %copy-done.3), kind=kOutput, calls=%fused_computation | convolution fusion | flops 10737418240 | bytes 24117248 | tf_op jit(solution)/shard_map/dot_general | solution.py:818
  711.1 69.0 %shard_map.113 = (bf16[512,1024]{1,0:T(8,128)(2,1)}, bf16[2048,2048]{1,0:T(8,128)(2,1)}) custom-call(f32[2048,1280]{1,0:T(8,128)} %convolution_bitcast_fusion.partial), custom_call_target="tpu_custom_call" | custom-call | tf_op jit(solution)/shard_map/pallas_call | solution.py:820
  780.1 22.2 %shard_map.114 = bf16[512,1024]{1,0:T(8,128)(2,1)} custom-call(s32[1]{0:T(128)} %bitcast.3.first, bf16[512,1024]{1,0:T(8,128)(2,1)} %get-tuple-element.18.queries, bf16[2048,2048]{1,0:T(8,128)(2,1)} %get-tuple-element.19.joint), custom_call_target="tpu_custom_call" | custom-call | tf_op jit(solution)/shard_map/pallas_call | solution.py:731
Async XLA Ops:
  7.2 687.3 %all-gather.2.cloned.1.call-start = ((), (), s32[]{:S(2)}) async-start(), calls=%async_computation | async-start | bytes 9437184 | tf_op jit(solution)/shard_map/all_gather | solution.py:762
  7.9 0.8 copy-start.1
  8.7 0.7 copy-start.2
  658.3 4.0 copy-start
  689.9 3.6 copy-start.3
Sparse Core Ops, SparseCore 0:
  10.1 225.0 all-gather.1

commit v3 on v2

--- a/solution.py
+++ b/solution.py
@@ -490,9 +490,18 @@
         gather.finish()
 
 
-def spread_kernel(sections, expanded, whole, expanded_sems, local_sems):
+def spread_kernel(
+    sections,
+    expanded,
+    hidden,
+    whole,
+    all_hidden,
+    expanded_sems,
+    hidden_sems,
+    local_sems,
+):
     p = Place(sections)
-    rows = expanded.shape[0]
+    rows, tokens = expanded.shape[0], hidden.shape[0]
     wide = TensorGather(
         p,
         expanded,
@@ -500,8 +509,34 @@
         expanded_sems,
         local_sems.at[0],
     )
+    wide_tokens = tokens // 8
+    half = (tokens - wide_tokens) // 2
+    states = [
+        SectionGather(
+            p,
+            hidden.at[pl.ds(first, size)],
+            lambda s, first=first, size=size: all_hidden.at[
+                pl.ds(pl.multiple_of(s * tokens + first, 16), size)
+            ],
+            hidden_sems.at[index],
+            local_sems.at[1 + index],
+            wide=index == 0,
+        )
+        for index, (first, size) in enumerate(
+            ((0, wide_tokens), (wide_tokens, half), (wide_tokens + half, half))
+        )
+    ]
     wide.start()
+    for one in states:
+        one.start()
+    for one in states:
+        one.cross()
+    for hop in range(1, p.count):
+        for one in states:
+            one.step(hop)
     wide.forward()
+    for one in states:
+        one.finish()
     wide.finish()
 
 
@@ -759,7 +794,6 @@
     head_cols = width_query.shape[0]
     kv_head_cols = width_kv.shape[0]
 
-    all_hidden = lax.all_gather(hidden, "section", axis=0, tiled=True)
     mixed_query, mixed_key, mixed_value, query_width, kv_width, fragment = pl.pallas_call(
         functools.partial(mix_kernel, sections),
         out_shape=[
@@ -801,18 +835,22 @@
         axis=1,
     )
     joined_cols = expanded.shape[1]
-    tokens = all_hidden.shape[0]
-
-    whole = pl.pallas_call(
+    token_part, feature_cols = hidden.shape
+    tokens = token_part * sections
+
+    whole, all_hidden = pl.pallas_call(
         functools.partial(spread_kernel, sections),
-        out_shape=jax.ShapeDtypeStruct((rows * tensors, joined_cols), bf16),
-        in_specs=[ANY],
-        out_specs=ANY,
-        scratch_shapes=[dma((6,)), dma((1,))],
+        out_shape=[
+            jax.ShapeDtypeStruct((rows * tensors, joined_cols), bf16),
+            jax.ShapeDtypeStruct((tokens, feature_cols), bf16),
+        ],
+        in_specs=[ANY] * 2,
+        out_specs=[ANY] * 2,
+        scratch_shapes=[dma((6,)), dma((3, 4, sections)), dma((4,))],
         compiler_params=pltpu.CompilerParams(
             vmem_limit_bytes=16 * MIB, has_side_effects=True
         ),
-    )(expanded)
+    )(expanded, hidden)
 
     grown = jnp.dot(fragment, whole, preferred_element_type=jnp.float32).astype(bf16)
     partial = jnp.dot(all_hidden, grown, preferred_element_type=jnp.float32)

time: 809 us -> 714 us (0.88)
  Pallas kernels: 721 us -> 648 us
  between operations: 14.1 us -> 0.73 us
    pallas_call x1, Pallas kernels: 536 us -> 439 us  [fast_device(): pl.pallas_call(functools.partial(mix_kernel, sections), out_shape=[jax.Sh...]
    pallas_call x1, Pallas kernels: 94.1 us -> 117 us  [fast_device(): pl.pallas_call(functools.partial(spread_kernel, sections), out_shape=[jax...]
  transfers between devices with their start and end apart: 1 -> 0, of which waited for: 0 -> 0; matrix products, arithmetic and copies ran while one was open for 6% -> 0% of each run, Pallas kernels for 78% -> 0%
where the time goes in v3:
time: 714 us
  Pallas kernels  648 us (91%)
  matrix products  56.7 us (8%)
  local copies, waits for them, and re-layouts  8.4 us (1%)
    pallas_call x1, Pallas kernels, fast_device(): pl.pallas_call(functools.partial(mix_kernel, sections), out_shape=[jax.Sh...  439 us
    pallas_call x1, Pallas kernels, fast_device(): pl.pallas_call(functools.partial(spread_kernel, sections), out_shape=[jax...  117 us
    pallas_call x1, Pallas kernels, fast_device(): pl.pallas_call(functools.partial(sum_kernel, sections), out_shape=[jax.Sh...  69.8 us
    dot_general x1, matrix products, fast_device(): jnp.dot(fragment, whole, preferred_element_type=jnp.float32).astype(bf16)  24.8 us
    pallas_call x1, Pallas kernels, attend(): pl.pallas_call(attend_kernel, out_shape=jax.ShapeDtypeStruct((rows, cols)...  22.3 us
    dot_general x3, matrix products, contract_last(): lax.dot_general(left_side, right_side, (((1,), (1,)), ((), ())), preferre...  18.3 us

profile of v3, /device:TPU:21, one launch (start us, length us, event | category | flops | bytes accessed | tf_op | source)
XLA Modules:
  0.0 713.6 jit_solution(10625044483535338565)
XLA Ops:
  0.6 0.0 copy-start.1
  0.6 0.8 copy-done.1
  1.5 0.0 copy-start.2
  1.5 0.7 copy-done.2
  2.1 438.8 %shard_map.111 = (bf16[1024,4096]{1,0:T(8,128)(2,1)}, bf16[1024,1024]{1,0:T(8,128)(2,1)}, bf16[1024,1024]{1,0:T(8,128)(2,1)}, bf16[1024,4096]{1,0:T(8,128)(2,1)}...) custom-call(f32[8]{0:T(128)S(1)} %copy-done.2, bf16[1024,4096]{1,0:T(8,128)(2,1)} %bitcast.14, ...), custom_call_target="tpu_custom_call" | custom-call | tf_op jit(solution)/shard_map/pallas_call | solution.py:797
  440.9 2.3 convolution_convert_fusion.3
  443.2 2.3 convolution_convert_fusion.2
  445.5 13.7 %convolution_convert_fusion.1 = bf16[1024,1024]{1,0:T(8,128)(2,1)S(1)} fusion(bf16[1024,4096]{1,0:T(8,128)(2,1)} %get-tuple-element.15, bf16[1024,4096]{1,0:T(8,128)(2,1)} %get-tuple-element.16), kind=kOutput, calls=%fused_computation.2 | convolution fusion | flops 8590983168 | bytes 18874368 | tf_op jit(solution)/shard_map/dot_general | solution.py:18
  459.3 0.0 copy-start
  459.3 0.2 pad_maximum_fusion.expanded
  459.5 1.0 copy-done
  460.5 116.7 %shard_map.112 = (bf16[4096,1280]{1,0:T(8,128)(2,1)S(1)}, bf16[2048,2048]{1,0:T(8,128)(2,1)S(1)}) custom-call(bf16[1024,1280]{1,0:T(8,128)(2,1)S(1)} %pad_maximum_fusion.expanded, bf16[256,2048]{1,0:T(8,128)(2,1)S(1)} %copy-done), custom_call_target="tpu_custom_call" | custom-call | tf_op jit(solution)/shard_map/pallas_call | solution.py:841
  577.2 24.8 %convolution_convert_fusion = bf16[2048,1280]{1,0:T(8,128)(2,1)S(1)} fusion(bf16[2048,4096]{1,0:T(8,128)(2,1)} %get-tuple-element.14, bf16[4096,1280]{1,0:T(8,128)(2,1)S(1)} %get-tuple-element.20), kind=kOutput, calls=%fused_computation | convolution fusion | flops 21477457920 | bytes 32505856 | tf_op jit(solution)/shard_map/dot_general | solution.py:855
  602.0 0.0 copy-start.3
  602.0 2.3 copy-done.3
  604.3 13.5 %fusion.1.partial = f32[2048,1280]{1,0:T(8,128)} fusion(bf16[2048,2048]{1,0:T(8,128)(2,1)S(1)} %get-tuple-element.21, bf16[2048,1280]{1,0:T(8,128)(2,1)S(1)} %convolution_convert_fusion), kind=kOutput, calls=%fused_computation.6 | convolution fusion | flops 10737418240 | bytes 24117248 | tf_op jit(solution)/shard_map/dot_general | solution.py:856
  617.8 69.8 %shard_map.113 = (bf16[512,1024]{1,0:T(8,128)(2,1)}, bf16[2048,2048]{1,0:T(8,128)(2,1)}) custom-call(f32[2048,1280]{1,0:T(8,128)} %fusion.1.partial), custom_call_target="tpu_custom_call" | custom-call | tf_op jit(solution)/shard_map/pallas_call | solution.py:858
  687.6 0.0 copy-start.4
  687.6 22.3 %shard_map.114 = bf16[512,1024]{1,0:T(8,128)(2,1)} custom-call(s32[1]{0:T(128)} %bitcast.3.first, bf16[512,1024]{1,0:T(8,128)(2,1)} %get-tuple-element.22.queries, bf16[2048,2048]{1,0:T(8,128)(2,1)} %get-tuple-element.23.joint), custom_call_target="tpu_custom_call" | custom-call | tf_op jit(solution)/shard_map/pallas_call | solution.py:766
  709.9 0.0 copy-done.4
  709.9 1.0 fusion
  711.0 2.6 slice.12
Async XLA Ops:
  0.6 0.8 copy-start.1
  1.5 0.7 copy-start.2
  459.3 1.2 copy-start
  602.0 2.3 copy-start.3
  687.6 22.3 %copy-start.4 = (bf16[2048,1280]{1,0:T(8,128)(2,1)S(1)}, bf16[2048,1280]{1,0:T(8,128)(2,1)}, u32[]{:S(2)}) copy-start(bf16[2048,1280]{1,0:T(8,128)(2,1)} %copy-done.3) | copy-start | bytes 15728644
